TPU v7x, 32 devices: a whole 2x2x4 slice. The times are simulated.
32 devices in a mesh: groups: 1, ctx: 32 (over z, y, x, core).
Axes of the slice: x: 2, y: 2, z: 4, core: 2. Of those that a mesh axis runs over, the one named last changes fastest.
Arguments:
- hidden: bfloat16 [9216, 5120], P(('groups', 'ctx')), may hold values from -6 to 6
- key_weight: bfloat16 [5120, 512], replicated, may hold values from -0.078125 to 0.078125
- value_weight: bfloat16 [5120, 512], replicated, may hold values from -0.078125 to 0.078125
- key_gain: float32 [128], replicated, may hold values from 0.1 to 1.9
- lengths: int32 [8], P('groups'), may hold values from 1 to 2304, 9216 in all
- dest_rows: int32 [8], P('groups'), may hold values from 0 to 7, each once
- queries: bfloat16 [32, 32, 128], P(('groups', 'ctx')), may hold values from -240 to 240
- new_keys: bfloat16 [32, 4, 128], P(('groups', 'ctx')), may hold values from -6 to 6
- new_values: bfloat16 [32, 4, 128], P(('groups', 'ctx')), may hold values from -6 to 6
Outputs:
- attended: bfloat16 [32, 32, 128], P(('groups', 'ctx'))
Inputs may be any that keep to these rules, and one draw needn't show every extreme that they name: The prompts' lengths sum to 9216 and the longest is exactly 2304. `dest_rows`: every decode row receives exactly one prompt.
All inputs are finite; a program needn't handle non-finite values.
Results may differ from a plain program's by a relative error of at most 0.012.
The roundings to bfloat16 on the way count: a program that leaves them out, or rounds other values in their place, can miss the bound.
Values may be sent and summed in bfloat16 or wider, within the bound.
A program may use at most 64 MiB of HBM per device.

v0:
```python
import jax
import jax.numpy as jnp
from jax import lax
from jax.sharding import PartitionSpec as P

KVH = 4
HD = 128
QPK = 8


ROPE_BASE = 1000000.0
EPS = 1e-06
NEG = -1e30


def rotate(normed, positions):
    half = normed.shape[-1] // 2
    freq = ROPE_BASE ** (-2.0 * jnp.arange(half, dtype=jnp.float32) / normed.shape[-1])
    angle = positions.astype(jnp.float32)[:, None] * freq[None, :]
    cosine = jnp.cos(angle)[:, None, :]
    sine = jnp.sin(angle)[:, None, :]
    first = normed[..., :half]
    second = normed[..., half:]
    return jnp.concatenate([first * cosine - second * sine, second * cosine + first * sine], -1)


def prompt_tables(lengths, dest_rows):
    ends = jnp.cumsum(lengths)
    starts = ends - lengths
    prompts = jnp.arange(lengths.shape[0], dtype=jnp.int32)
    owner = jnp.sum(jnp.where(dest_rows[None, :] == prompts[:, None], prompts[None, :], 0), 1)
    return (starts, ends, owner)


def near_part(query, fresh_keys):
    scale = 1.0 / HD**0.5
    near = jnp.dot(query, fresh_keys.T, preferred_element_type=jnp.float32) * scale
    step_of = jnp.arange(query.shape[0], dtype=jnp.int32) // QPK
    allowed = jnp.arange(fresh_keys.shape[0], dtype=jnp.int32)[None, :] <= step_of[:, None]
    return (jnp.where(allowed, near, NEG), allowed)


def attend(query, cache_keys, cache_values, live, fresh_keys, fresh_values):
    scale = 1.0 / HD**0.5
    far = jnp.dot(query, cache_keys.T, preferred_element_type=jnp.float32) * scale
    far = jnp.where(live[None, :], far, NEG)
    near, allowed = near_part(query, fresh_keys)
    top = jnp.maximum(jnp.max(far, -1), jnp.max(near, -1))[:, None]
    far_weights = jnp.where(live[None, :], jnp.exp(far - top), 0.0)
    near_weights = jnp.where(allowed, jnp.exp(near - top), 0.0)
    total = jnp.sum(far_weights, -1) + jnp.sum(near_weights, -1)
    mixed = jnp.dot(
        far_weights.astype(jnp.bfloat16), cache_values, preferred_element_type=jnp.float32
    )
    mixed = mixed + jnp.dot(
        near_weights.astype(jnp.bfloat16), fresh_values, preferred_element_type=jnp.float32
    )
    return (mixed / total[:, None]).astype(jnp.bfloat16)


def own_prompt(myself, prompts, owner, starts, lengths):
    my_row = myself // KVH
    row_pick = prompts == my_row
    prompt = jnp.sum(jnp.where(row_pick, owner, 0))
    prompt_pick = prompts == prompt
    start = jnp.sum(jnp.where(prompt_pick, starts, 0))
    length = jnp.sum(jnp.where(prompt_pick, lengths, 0))
    return (start, length)


def local(
    hidden, key_weight, value_weight, key_gain, lengths, dest_rows, queries, new_keys, new_values
):
    devices = lax.axis_size("ctx")
    myself = lax.axis_index("ctx")
    tok_count = hidden.shape[0]
    row_count = lengths.shape[0]
    capacity = tok_count * devices // 4
    starts, ends, owner = prompt_tables(lengths, dest_rows)
    prompts = jnp.arange(row_count, dtype=jnp.int32)
    stream = myself * tok_count + jnp.arange(tok_count, dtype=jnp.int32)
    prompt_of = jnp.sum((stream[:, None] >= ends[None, :]).astype(jnp.int32), 1)
    onehot = prompt_of[:, None] == prompts[None, :]
    positions = stream - jnp.sum(jnp.where(onehot, starts[None, :], 0), 1)
    raw = jnp.dot(hidden, key_weight, preferred_element_type=jnp.float32).reshape(
        tok_count, KVH, HD
    )
    normed = raw * lax.rsqrt(jnp.mean(raw * raw, -1, keepdims=True) + EPS) * key_gain
    keys_tok = rotate(normed, positions).astype(jnp.bfloat16)
    values_tok = jnp.dot(hidden, value_weight, preferred_element_type=jnp.float32).astype(
        jnp.bfloat16
    )
    width = KVH * HD
    spread_rows = (tok_count + devices - 1) // devices + 1
    slot_rows = capacity // devices
    zero_int = jnp.int32(0)
    offset_now = myself * tok_count % devices
    empty_lay = jnp.zeros((spread_rows * devices, width), jnp.bfloat16)
    laid_keys = lax.dynamic_update_slice(
        empty_lay, keys_tok.reshape(tok_count, width), (offset_now, zero_int)
    ).reshape(spread_rows, devices, width)
    laid_values = lax.dynamic_update_slice(empty_lay, values_tok, (offset_now, zero_int)).reshape(
        spread_rows, devices, width
    )
    mid_keys, mid_values = (
        lax.all_to_all(laid_keys, "ctx", split_axis=1, concat_axis=1, tiled=True),
        lax.all_to_all(laid_values, "ctx", split_axis=1, concat_axis=1, tiled=True),
    )
    column = jnp.arange(tok_count, dtype=jnp.int32)
    global_tok = myself + devices * column
    source = global_tok // tok_count
    inside = global_tok % tok_count
    source_offset = source * tok_count % devices
    lane = (inside + source_offset - myself) // devices
    pick_mid = lane * devices + source
    blank_mid = jnp.zeros((slot_rows * KVH, HD), jnp.bfloat16)
    table_keys = jnp.concatenate(
        [
            mid_keys.reshape(spread_rows * devices, KVH, HD)[pick_mid].reshape(tok_count * KVH, HD),
            blank_mid,
        ],
        0,
    )
    table_values = jnp.concatenate(
        [
            mid_values.reshape(spread_rows * devices, KVH, HD)[pick_mid].reshape(
                tok_count * KVH, HD
            ),
            blank_mid,
        ],
        0,
    )
    slots = jnp.arange(devices, dtype=jnp.int32)
    slot_row = slots // KVH
    slot_head = slots % KVH
    row_match = slot_row[:, None] == prompts[None, :]
    slot_prompt = jnp.sum(jnp.where(row_match, owner[None, :], 0), 1)
    prompt_match = slot_prompt[:, None] == prompts[None, :]
    slot_start = jnp.sum(jnp.where(prompt_match, starts[None, :], 0), 1)
    slot_length = jnp.sum(jnp.where(prompt_match, lengths[None, :], 0), 1)
    residue = (myself - slot_start) % devices
    first_index = (slot_start + residue - myself) // devices
    steps_along = jnp.arange(slot_rows, dtype=jnp.int32)
    tok_index = first_index[:, None] + steps_along[None, :]
    place = residue[:, None] + devices * steps_along[None, :]
    usable = (place < slot_length[:, None])[..., None]
    pick_slot = tok_index * KVH + slot_head[:, None]
    nothing = jnp.zeros((), jnp.bfloat16)
    send_keys = jnp.where(usable, table_keys[pick_slot], nothing)
    send_values = jnp.where(usable, table_values[pick_slot], nothing)
    came_keys, came_values = (
        lax.all_to_all(send_keys, "ctx", split_axis=0, concat_axis=0, tiled=True),
        lax.all_to_all(send_values, "ctx", split_axis=0, concat_axis=0, tiled=True),
    )
    start, length = own_prompt(myself, prompts, owner, starts, lengths)
    position_all = jnp.arange(capacity, dtype=jnp.int32)
    sender = (position_all % devices + start) % devices
    pick_cache = sender * slot_rows + position_all // devices
    cache_keys = came_keys.reshape(devices * slot_rows, HD)[pick_cache]
    cache_values = came_values.reshape(devices * slot_rows, HD)[pick_cache]
    live = position_all < length
    output = attend(queries[0], cache_keys, cache_values, live, new_keys[0], new_values[0])
    return output[None]


def solution(mesh):
    placed = (
        P(("groups", "ctx"), None),
        P(),
        P(),
        P(),
        P("groups"),
        P("groups"),
        P(("groups", "ctx"), None, None),
        P(("groups", "ctx"), None, None),
        P(("groups", "ctx"), None, None),
    )
    return jax.shard_map(
        local,
        mesh=mesh,
        in_specs=placed,
        out_specs=P(("groups", "ctx"), None, None),
        check_vma=False,
    )
```

profile of v0, /device:TPU:0, one launch (start us, length us, event | category | flops | bytes accessed | tf_op | source)
XLA Modules:
  0.0 129.3 jit_solution(5895604654068349280)
XLA Ops:
  0.0 0.0 copy-start
  0.0 0.9 select_reduce_fusion.4
  1.0 0.8 reduce-window.8
  1.8 0.6 fusion.33
  2.4 2.0 %fusion.32 = (s32[]{:T(128)}, s32[8]{0:T(128)S(1)}, s32[]{:T(128)}) fusion(s32[]{:T(128)} %fusion.33, s32[8]{0:T(128)} %param.13, s32[8,1]{0,1:T(1,128)S(1)} %reduce-window.8), kind=kLoop, calls=%fused_computation.108 | loop fusion | flops 46 | bytes 108 | tf_op jit(solution)/shard_map/reduce_sum | solution.py:66
  4.4 0.1 convert_reduce_fusion
  4.5 0.1 select_reduce_fusion
  4.6 0.0 copy-done.6
  4.6 0.0 copy-done
  4.6 0.0 copy-start.5
  4.6 5.0 %fusion.39 = f32[288,512]{1,0:T(8,128)} fusion(bf16[288,5120]{1,0:T(8,128)(2,1)S(1)} %copy-done, bf16[5120,512]{1,0:T(8,128)(2,1)} %param.10), kind=kOutput, calls=%fused_computation.118 | convolution fusion | flops 1509949440 | bytes 8781824 | tf_op jit(solution)/shard_map/dot_general | solution.py:85
  9.6 1.3 reshape.575
  10.9 0.4 multiply_reduce_fusion
  11.2 0.7 add_rsqrt_fusion
  11.9 0.6 multiply_cosine_fusion
  12.5 0.0 copy-done.5
  12.5 1.3 multiply_multiply_fusion
  13.8 0.6 subtract_convert_fusion
  14.4 0.4 pad_maximum_fusion
  14.9 1.0 copy.25
  15.9 7.3 %all-to-all-start = ((bf16[10,32,512]{2,0,1:T(8,128)(2,1)}), bf16[10,32,512]{2,0,1:T(8,128)(2,1)S(1)}, u32[]{:S(2)}, u32[]{:S(2)}) async-start(bf16[10,32,512]{2,0,1:T(8,128)(2,1)} %copy.25), calls=%async_computation | async-start | bytes 1048576 | tf_op jit(solution)/shard_map/all_to_all | solution.py:106
  23.2 0.0 copy-start.7
  23.2 0.0 copy-start.4
  23.2 4.2 %fusion.1 = bf16[320,512]{1,0:T(8,128)(2,1)S(1)} fusion(bf16[320,512]{1,0:T(8,128)(2,1)S(1)} %broadcast_in_dim.154.clone.1, s32[]{:T(128)S(6)} %select_n.237, bf16[288,5120]{1,0:T(8,128)(2,1)S(1)} %copy-done, bf16[5120,512]{1,0:T(8,128)(2,1)} %param.11), kind=kOutput, calls=%fused_computation.9 | convolution fusion | flops 1510096896 | bytes 8486916 | tf_op jit(solution)/shard_map/dot_general | solution.py:90
  27.4 1.0 copy.27
  28.4 0.0 copy-done.7
  28.4 0.1 select_reduce_fusion.3
  28.5 0.0 copy-done.4
  28.5 0.1 select_reduce_fusion.1
  28.6 10.1 %all-to-all-done = bf16[10,32,512]{2,0,1:T(8,128)(2,1)S(1)} async-done(((bf16[10,32,512]{2,0,1:T(8,128)(2,1)}), bf16[10,32,512]{2,0,1:T(8,128)(2,1)S(1)}, u32[]{:S(2)}, u32[]{:S(2)}) %all-to-all-start) | async-done | bytes 327712 | tf_op jit(solution)/shard_map/all_to_all | solution.py:106
  38.7 3.3 %all-to-all-start.2 = ((bf16[10,32,512]{2,0,1:T(8,128)(2,1)}), bf16[10,32,512]{2,0,1:T(8,128)(2,1)}, u32[]{:S(2)}, u32[]{:S(2)}) async-start(bf16[10,32,512]{2,0,1:T(8,128)(2,1)} %copy.27), calls=%async_computation.2 | async-start | bytes 1048576 | tf_op jit(solution)/shard_map/all_to_all | solution.py:107
  42.1 0.1 compare_select_fusion.1
  42.1 0.1 reshape.594
  42.2 0.1 fusion.21
  42.3 0.1 add_compare_fusion
  42.4 0.9 copy.26
  43.3 1.8 %reshape.577 = bf16[320,4,128]{2,1,0:T(4,128)(2,1)} reshape(bf16[10,32,512]{2,1,0:T(8,128)(2,1)} %copy.26) | data formatting | bytes 655360 | tf_op jit(solution)/shard_map/reshape | solution.py:119
  45.1 12.5 %all-to-all-done.2 = bf16[10,32,512]{2,0,1:T(8,128)(2,1)} async-done(((bf16[10,32,512]{2,0,1:T(8,128)(2,1)}), bf16[10,32,512]{2,0,1:T(8,128)(2,1)}, u32[]{:S(2)}, u32[]{:S(2)}) %all-to-all-start.2) | async-done | bytes 327712 | tf_op jit(solution)/shard_map/all_to_all | solution.py:107
  57.6 1.2 copy.28
  58.8 0.8 reshape.581
  59.6 2.8 %gather_fusion = bf16[288,4,128]{2,1,0:T(4,128)(2,1)} fusion(bf16[320,4,128]{2,1,0:T(4,128)(2,1)} %reshape.577, s32[1024]{0:T(1024)S(1)} %pad_clamp_fusion.2), kind=kCustom, calls=%fused_computation | custom fusion | bytes 590976 | tf_op jit(solution)/shard_map/gather | solution.py:119
  62.3 2.8 %gather_fusion.3 = bf16[288,4,128]{2,1,0:T(4,128)(2,1)} fusion(bf16[320,4,128]{2,1,0:T(4,128)(2,1)} %reshape.581, s32[1024]{0:T(1024)S(1)} %pad_clamp_fusion.2), kind=kCustom, calls=%fused_computation.3 | custom fusion | bytes 590976 | tf_op jit(solution)/shard_map/gather | solution.py:126
  65.1 1.0 concatenate.11
  66.1 5.6 %gather_fusion.1 = bf16[2304,128]{1,0:T(8,128)(2,1)} fusion(bf16[1440,128]{1,0:T(8,128)(2,1)S(1)} %concatenate.11, s32[3072]{0:T(1024)S(1)} %pad_clamp_fusion.1), kind=kCustom, calls=%fused_computation.1 | custom fusion | bytes 1188864 | tf_op jit(solution)/shard_map/gather | solution.py:149
  71.7 1.0 concatenate.12
  72.7 5.6 %gather_fusion.4 = bf16[2304,128]{1,0:T(8,128)(2,1)} fusion(bf16[1440,128]{1,0:T(8,128)(2,1)S(1)} %concatenate.12, s32[3072]{0:T(1024)S(1)} %pad_clamp_fusion.1), kind=kCustom, calls=%fused_computation.4 | custom fusion | bytes 1188864 | tf_op jit(solution)/shard_map/gather | solution.py:150
  78.2 2.2 %broadcast_select_fusion.1 = (bf16[32,72,128]{2,1,0:T(8,128)(2,1)S(1)}, bf16[32,72,128]{2,1,0:T(8,128)(2,1)}) fusion(bf16[32,72,128]{2,1,0:T(8,128)(2,1)} %bitcast.44, pred[32,72]{1,0:T(8,128)(4,1)S(1)} %add_compare_fusion, bf16[32,72,128]{2,1,0:T(8,128)(2,1)} %bitcast.45), kind=kLoop, calls=%fused_computation.21 | loop fusion | flops 589824 | bytes 2361600 | tf_op jit(solution)/shard_map/jit(_where)/select_n | solution.py:149
  80.4 19.6 %all_to_all.20 = bf16[32,72,128]{2,1,0:T(8,128)(2,1)} all-to-all(bf16[32,72,128]{2,1,0:T(8,128)(2,1)S(1)} %get-tuple-element.13), channel_id=1, replica_groups=mesh['groups'=1,'ctx'=32] {'ctx'}, dimensions={0} | all-to-all | bytes 1179648 | tf_op jit(solution)/shard_map/all_to_all | solution.py:152
  100.0 3.3 %all-to-all-start.3 = ((bf16[32,72,128]{2,1,0:T(8,128)(2,1)}), bf16[32,72,128]{2,1,0:T(8,128)(2,1)S(1)}, u32[]{:S(2)}, u32[]{:S(2)}) async-start(bf16[32,72,128]{2,1,0:T(8,128)(2,1)} %get-tuple-element.14), calls=%async_computation.3 | async-start | bytes 1179648 | tf_op jit(solution)/shard_map/all_to_all | solution.py:153
  103.4 0.7 fusion.13
  104.1 0.0 copy-start.3
  104.1 0.6 iota_compare_fusion.1
  104.7 0.0 copy-done.3
  104.7 1.9 %fusion.38 = (f32[32]{0:T(128)}, f32[32,4]{0,1:T(4,128)}) fusion(bf16[1,4,128]{2,1,0:T(4,128)(2,1)} %param.16, bf16[1,32,128]{2,1,0:T(8,128)(2,1)} %param.15, s32[32]{0:T(128)S(1)} %and_select_fusion.7), kind=kOutput, calls=%fused_computation.117 | convolution fusion | flops 33248 | bytes 9984 | tf_op jit(solution)/shard_map/dot_general | solution.py:37
  106.6 6.2 %gather_fusion.2 = bf16[2304,128]{1,0:T(8,128)(2,1)} fusion(bf16[2304,128]{1,0:T(8,128)(2,1)} %bitcast.43, s32[3072]{0:T(1024)S(1)} %pad_clamp_fusion), kind=kCustom, calls=%fused_computation.2 | custom fusion | bytes 1188864 | tf_op jit(solution)/shard_map/gather | solution.py:159
  112.8 1.5 %fusion.37 = (f32[32]{0:T(128)S(1)}, f32[2304,32]{0,1:T(8,128)S(1)}) fusion(bf16[2304,128]{1,0:T(8,128)(2,1)} %gather_fusion.2, bf16[1,32,128]{2,1,0:T(8,128)(2,1)} %param.15, pred[2304]{0:T(1024)(128)(4,1)S(1)} %iota_compare_fusion.1), kind=kOutput, calls=%fused_computation.116 | convolution fusion | flops 19095520 | bytes 895360 | tf_op jit(solution)/shard_map/dot_general | solution.py:45
  114.3 0.7 max.7
  115.0 1.3 fusion.23
  116.3 0.7 fusion.6
  117.0 3.1 %all-to-all-done.3 = bf16[32,72,128]{2,1,0:T(8,128)(2,1)S(1)} async-done(((bf16[32,72,128]{2,1,0:T(8,128)(2,1)}), bf16[32,72,128]{2,1,0:T(8,128)(2,1)S(1)}, u32[]{:S(2)}, u32[]{:S(2)}) %all-to-all-start.3) | async-done | bytes 589856 | tf_op jit(solution)/shard_map/all_to_all | solution.py:153
  120.1 5.6 %gather_fusion.5 = bf16[2304,128]{1,0:T(8,128)(2,1)} fusion(bf16[2304,128]{1,0:T(8,128)(2,1)S(1)} %bitcast.42, s32[3072]{0:T(1024)S(1)} %pad_clamp_fusion), kind=kCustom, calls=%fused_computation.5 | custom fusion | bytes 1188864 | tf_op jit(solution)/shard_map/gather | solution.py:160
  125.6 1.4 %fusion.8 = f32[32,128]{1,0:T(8,128)S(1)} fusion(bf16[2304,128]{1,0:T(8,128)(2,1)} %gather_fusion.5, f32[2304,32]{0,1:T(8,128)} %copy-done.1, f32[32]{0:T(128)} %copy-done.2, pred[2304]{0:T(1024)(128)(4,1)S(1)} %iota_compare_fusion.1), kind=kOutput, calls=%fused_computation.29 | convolution fusion | flops 19095552 | bytes 903552 | tf_op jit(solution)/shard_map/dot_general | solution.py:52
  127.1 0.7 add.339
  127.8 1.5 %fusion.4 = bf16[1,32,128]{2,1,0:T(8,128)(2,1)} fusion(f32[32,128]{1,0:T(8,128)S(1)} %fusion.8, f32[32]{0:T(128)S(1)} %add.339, f32[32,4]{0,1:T(4,128)} %get-tuple-element.21, bf16[1,4,128]{2,1,0:T(4,128)(2,1)} %param.17, f32[32]{0:T(128)} %copy-done.2, s32[32]{0:T(128)} %copy-done.3), kind=kOutput, calls=%fused_computation.13 | convolution fusion | flops 45568 | bytes 26496 | tf_op jit(solution)/shard_map/dot_general | solution.py:55
  (18 shorter events, 0.2 us)
Async XLA Ops:
  0.0 4.6 %copy-start = (bf16[288,5120]{1,0:T(8,128)(2,1)S(1)}, bf16[288,5120]{1,0:T(8,128)(2,1)}, u32[]{:S(2)}) copy-start(bf16[288,5120]{1,0:T(8,128)(2,1)} %param.9) | copy-start | bytes 8847364
  1.0 3.6 %copy-start.6 = (s32[8]{0:T(128)}, s32[8]{0:T(128)S(1)}, u32[]{:S(2)}) copy-start(s32[8]{0:T(128)S(1)} %select_reduce_fusion.4) | copy-start | bytes 100
  4.6 7.9 %copy-start.5 = (f32[128]{0:T(128)S(1)}, f32[128]{0:T(128)}, u32[]{:S(2)}) copy-start(f32[128]{0:T(128)} %param.12) | copy-start | bytes 1540
  15.9 22.9 %all-to-all-start = ((bf16[10,32,512]{2,0,1:T(8,128)(2,1)}), bf16[10,32,512]{2,0,1:T(8,128)(2,1)S(1)}, u32[]{:S(2)}, u32[]{:S(2)}) async-start(bf16[10,32,512]{2,0,1:T(8,128)(2,1)} %copy.25), calls=%async_computation | async-start | bytes 1048576 | tf_op jit(solution)/shard_map/all_to_all | solution.py:106
  23.2 5.2 %copy-start.7 = (s32[8]{0:T(128)S(1)}, s32[8]{0:T(128)}, u32[]{:S(2)}) copy-start(s32[8]{0:T(128)} %copy-done.6) | copy-start | bytes 100
  23.2 5.3 %copy-start.4 = (s32[8]{0:T(128)S(1)}, s32[8]{0:T(128)}, u32[]{:S(2)}) copy-start(s32[8]{0:T(128)} %param.13) | copy-start | bytes 100
  38.7 18.9 %all-to-all-start.2 = ((bf16[10,32,512]{2,0,1:T(8,128)(2,1)}), bf16[10,32,512]{2,0,1:T(8,128)(2,1)}, u32[]{:S(2)}, u32[]{:S(2)}) async-start(bf16[10,32,512]{2,0,1:T(8,128)(2,1)} %copy.27), calls=%async_computation.2 | async-start | bytes 1048576 | tf_op jit(solution)/shard_map/all_to_all | solution.py:107
  100.0 20.0 %all-to-all-start.3 = ((bf16[32,72,128]{2,1,0:T(8,128)(2,1)}), bf16[32,72,128]{2,1,0:T(8,128)(2,1)S(1)}, u32[]{:S(2)}, u32[]{:S(2)}) async-start(bf16[32,72,128]{2,1,0:T(8,128)(2,1)} %get-tuple-element.14), calls=%async_computation.3 | async-start | bytes 1179648 | tf_op jit(solution)/shard_map/all_to_all | solution.py:153
  104.1 0.7 copy-start.3
  114.3 1.9 %copy-start.1 = (f32[2304,32]{0,1:T(8,128)}, f32[2304,32]{0,1:T(8,128)S(1)}, u32[]{:S(2)}) copy-start(f32[2304,32]{0,1:T(8,128)S(1)} %get-tuple-element.19) | copy-start | bytes 884740
  115.0 1.3 copy-start.2
where the time goes:
time: 130 us; the launch traced here: 129 us
  local copies, waits for them, and re-layouts  38.6 us (30%)
  waiting for transfers between devices  25.7 us (20%)
  blocking collectives  19.6 us (15%)
  other arithmetic  15.8 us (12%)
  matrix products  15.5 us (12%)
  starting transfers between devices  13.9 us (11%)
    all_to_all x1, blocking collectives, local(): lax.all_to_all(send_keys, 'ctx', split_axis=0, concat_axis=0, tiled=True)  19.6 us
    all_to_all x1, waiting for transfers between devices, local(): lax.all_to_all(laid_values, 'ctx', split_axis=1, concat_axis=1, tiled=True)  12.5 us
    all_to_all x1, waiting for transfers between devices, local(): lax.all_to_all(laid_keys, 'ctx', split_axis=1, concat_axis=1, tiled=True)  10.1 us
    all_to_all x1, starting transfers between devices, local(): lax.all_to_all(laid_keys, 'ctx', split_axis=1, concat_axis=1, tiled=True)  7.3 us
    gather x1, local copies, waits for them, and re-layouts, local(): cache_keys = came_keys.reshape(devices * slot_rows, HD)[pick_cache]  6.2 us
    gather x1, local copies, waits for them, and re-layouts, local(): send_keys = jnp.where(usable, table_keys[pick_slot], nothing)  5.57 us
    gather x1, local copies, waits for them, and re-layouts, local(): cache_values = came_values.reshape(devices * slot_rows, HD)[pick_cache]  5.56 us
    gather x1, local copies, waits for them, and re-layouts, local(): send_values = jnp.where(usable, table_values[pick_slot], nothing)  5.55 us
  transfers between devices with their start and end apart: 3, of which 3 were waited for; matrix products, arithmetic and copies ran while one was open for 17% of the time, Pallas kernels for 0%

commit v1 on v0

v1 whole, which is shorter than its diff:
```python
import functools

import jax
import jax.numpy as jnp
import numpy as np
from jax import lax
from jax.experimental import pallas as pl
from jax.experimental.pallas import tpu as pltpu
from jax.sharding import PartitionSpec as P

KVH = 4
HD = 128
QPK = 8
LANES = 128

ROPE_BASE = 1000000.0
EPS = 1e-06
NEG = -1e30
MESH = pl.DeviceIdType.MESH
CONTRACT_LAST = (((1,), (1,)), ((), ()))
CONTRACT_FIRST = (((0,), (0,)), ((), ()))


def kernel(
    n,
    rows,
    lengths,
    dest_rows,
    hidden,
    key_weight,
    value_weight,
    gain,
    freq,
    query,
    new_keys,
    new_values,
    out,
    hid_v,
    kw_v,
    vw_v,
    acc_k,
    acc_v,
    cos_v,
    sin_v,
    row_v,
    qbuf,
    o_send,
    s_send,
    o_recv,
    s_recv,
    near_k,
    near_v,
    mix_v,
    hid_sem,
    kw_sem,
    vw_sem,
    q_send_sem,
    q_recv_sem,
    o_send_sem,
    o_recv_sem,
    s_send_sem,
    s_recv_sem,
):
    me = lax.axis_index("ctx")
    my_row, my_head = me // KVH, me % KVH
    chunks, tok, depth = hid_v.shape
    nq = query.shape[1]
    scale = 1.0 / HD**0.5

    def chunk_copies(c):
        part = pl.ds(pl.multiple_of(c * depth, depth), depth)
        return (
            pltpu.make_async_copy(hidden.at[:, part], hid_v.at[c], hid_sem.at[c]),
            pltpu.make_async_copy(key_weight.at[part], kw_v.at[c], kw_sem.at[c]),
            pltpu.make_async_copy(value_weight.at[part], vw_v.at[c], vw_sem.at[c]),
        )

    barrier = pltpu.get_barrier_semaphore()

    @pl.loop(1, n)
    def _(i):
        pl.semaphore_signal(
            barrier, inc=1, device_id={"ctx": lax.rem(me + i, n)}, device_id_type=MESH
        )

    @pl.loop(0, chunks)
    def _(c):
        for copy in chunk_copies(c):
            copy.start()

    qbuf[my_head, my_row] = query[0]

    stream = me * tok + lax.broadcasted_iota(jnp.int32, (tok, LANES), 0)
    begin = jnp.int32(0)
    start_of = jnp.zeros((tok, LANES), jnp.int32)
    row_of = jnp.zeros((tok, LANES), jnp.int32)
    for p in range(rows):
        inside = stream >= begin
        start_of = jnp.where(inside, begin, start_of)
        row_of = jnp.where(inside, dest_rows[p], row_of)
        begin = begin + lengths[p]
    row_v[...] = row_of
    angle = (stream - start_of).astype(jnp.float32) * freq[...]
    cos_v[...] = jnp.cos(angle)
    sine = jnp.sin(angle)
    lane = lax.broadcasted_iota(jnp.int32, (tok, LANES), 1)
    sin_v[...] = jnp.where(lane < HD // 2, -sine, sine)

    pl.semaphore_wait(barrier, n - 1)

    def query_copy(d, s):
        return pltpu.make_async_remote_copy(
            src_ref=qbuf.at[my_head, my_row],
            dst_ref=qbuf.at[my_head, my_row],
            send_sem=q_send_sem.at[d],
            recv_sem=q_recv_sem.at[s],
            device_id={"ctx": d},
            device_id_type=MESH,
        )

    @pl.loop(1, n)
    def _(i):
        query_copy(lax.rem(me + i, n), me).start()

    steps = new_keys.shape[1]
    near_k[...] = jnp.zeros_like(near_k)
    near_v[...] = jnp.zeros_like(near_v)
    near_k[0:steps] = new_keys[0]
    near_v[0:steps] = new_values[0]
    own = jnp.concatenate([query[0]] * (LANES // nq), 0)
    near = lax.dot_general(near_k[...], own, CONTRACT_LAST, preferred_element_type=jnp.float32)
    near = near * scale
    u = lax.broadcasted_iota(jnp.int32, near.shape, 0)
    step_of = lax.broadcasted_iota(jnp.int32, near.shape, 1) % nq // QPK
    allowed = u <= jnp.minimum(step_of, steps - 1)
    near = jnp.where(allowed, near, NEG)
    near_top = jnp.max(near, 0, keepdims=True)
    near_w = jnp.where(allowed, jnp.exp(near - near_top), 0.0)
    near_sum = jnp.sum(near_w, 0, keepdims=True)
    near_o = lax.dot_general(
        near_w.astype(jnp.bfloat16), near_v[...], CONTRACT_FIRST, preferred_element_type=jnp.float32
    )[:nq]

    acc_k[...] = jnp.zeros_like(acc_k)
    acc_v[...] = jnp.zeros_like(acc_v)

    @pl.loop(0, chunks)
    def _(c):
        for copy in chunk_copies(c):
            copy.wait()
        h = hid_v[c]
        acc_k[...] += jnp.dot(h, kw_v[c], preferred_element_type=jnp.float32)
        acc_v[...] += jnp.dot(h, vw_v[c], preferred_element_type=jnp.float32)

    @pl.loop(1, n)
    def _(i):
        s = lax.rem(me + i, n)
        pltpu.make_async_remote_copy(
            src_ref=qbuf.at[my_head, my_row],
            dst_ref=qbuf.at[s % KVH, s // KVH],
            send_sem=q_send_sem.at[s],
            recv_sem=q_recv_sem.at[s],
            device_id={"ctx": s},
            device_id_type=MESH,
        ).wait_recv()

    def part_copies(r, h, d, s):
        return (
            pltpu.make_async_remote_copy(
                src_ref=o_send.at[h, r],
                dst_ref=o_recv.at[s],
                send_sem=o_send_sem.at[d],
                recv_sem=o_recv_sem.at[s],
                device_id={"ctx": d},
                device_id_type=MESH,
            ),
            pltpu.make_async_remote_copy(
                src_ref=s_send.at[h, r * nq // LANES],
                dst_ref=s_recv.at[s],
                send_sem=s_send_sem.at[d],
                recv_sem=s_recv_sem.at[s],
                device_id={"ctx": d},
                device_id_type=MESH,
            ),
        )

    wide = rows * nq
    column_row = lax.broadcasted_iota(jnp.int32, (tok, wide), 1) // nq
    row_of = jnp.concatenate([row_v[...]] * (wide // LANES), 1)
    live = row_of == column_row
    for h in range(KVH):
        cols = slice(h * HD, (h + 1) * HD)
        raw = acc_k[:, cols]
        normed = raw * lax.rsqrt(jnp.mean(raw * raw, -1, keepdims=True) + EPS) * gain[...]
        keys = normed * cos_v[...] + pltpu.roll(normed, HD // 2, 1) * sin_v[...]
        values = acc_v[:, cols].astype(jnp.bfloat16)
        far = lax.dot_general(
            keys.astype(jnp.bfloat16),
            qbuf[h].reshape(wide, HD),
            CONTRACT_LAST,
            preferred_element_type=jnp.float32,
        )
        far = jnp.where(live, far * scale, NEG)
        top = jnp.max(far, 0, keepdims=True)
        weights = jnp.where(live, jnp.exp(far - top), 0.0)
        total = jnp.sum(weights, 0, keepdims=True)
        mixed = lax.dot_general(
            weights.astype(jnp.bfloat16), values, CONTRACT_FIRST, preferred_element_type=jnp.float32
        )
        o_send[h] = mixed.astype(jnp.bfloat16).reshape(rows, nq, HD)
        for b in range(wide // LANES):
            block = slice(b * LANES, (b + 1) * LANES)
            s_send[h, b] = jnp.concatenate([top[:, block], total[:, block]], 0)

        @pl.loop(0, rows)
        def _(i):
            r = lax.rem(my_row + i, rows)
            d = r * KVH + h

            @pl.when(d != me)
            def _():
                for copy in part_copies(r, h, d, me):
                    copy.start()

    o_recv[me] = o_send[my_head, my_row]
    s_recv[me] = s_send[my_head, my_row * nq // LANES]

    @pl.loop(1, n)
    def _(i):
        s = lax.rem(me + i, n)
        for copy in part_copies(s // KVH, s % KVH, s, s):
            copy.wait_recv()

    tops, sums = s_recv[:, 0, :], s_recv[:, 1, :]
    best = jnp.maximum(jnp.max(tops, 0, keepdims=True), near_top)
    factor = jnp.exp(tops - best)
    near_factor = jnp.exp(near_top - best)
    total = jnp.sum(factor * sums, 0, keepdims=True) + near_factor * near_sum
    shares = jnp.concatenate(
        [
            factor / total,
            near_factor / total,
            jnp.zeros((LANES - n - 1, LANES), jnp.float32),
        ],
        0,
    )
    mix_v[...] = shares.T
    mine = mix_v[pl.ds(pl.multiple_of(lax.rem(my_row * nq, LANES), nq), nq), :]
    result = near_o * mine[:, n : n + 1]
    for s in range(n):
        result = result + o_recv[s].astype(jnp.float32) * mine[:, s : s + 1]
    out[0] = result.astype(jnp.bfloat16)

    @pl.loop(1, n)
    def _(i):
        d = lax.rem(me + i, n)
        query_copy(d, me).wait_send()
        for copy in part_copies(d // KVH, d % KVH, d, me):
            copy.wait_send()


def local(
    hidden, key_weight, value_weight, key_gain, lengths, dest_rows, queries, new_keys, new_values
):
    n = lax.axis_size("ctx")
    rows = lengths.shape[0]
    tok, width = hidden.shape
    nq = queries.shape[1]
    kv = KVH * HD
    depth = 512
    chunks = width // depth
    half = np.arange(HD // 2, dtype=np.float32)
    freq = np.power(np.float32(ROPE_BASE), np.float32(-2.0) * half / np.float32(HD))
    freq = jnp.asarray(np.concatenate([freq, freq])[None, :].astype(np.float32))
    vmem = pl.BlockSpec(memory_space=pltpu.VMEM)
    smem = pl.BlockSpec(memory_space=pltpu.SMEM)
    hbm = pl.BlockSpec(memory_space=pl.ANY)
    bf16, f32 = jnp.bfloat16, jnp.float32
    blocks = rows * nq // LANES
    return pl.pallas_call(
        functools.partial(kernel, n, rows),
        out_shape=jax.ShapeDtypeStruct((1, nq, HD), bf16),
        in_specs=[smem, smem, hbm, hbm, hbm, vmem, vmem, vmem, vmem, vmem],
        out_specs=vmem,
        scratch_shapes=[
            pltpu.VMEM((chunks, tok, depth), bf16),
            pltpu.VMEM((chunks, depth, kv), bf16),
            pltpu.VMEM((chunks, depth, kv), bf16),
            pltpu.VMEM((tok, kv), f32),
            pltpu.VMEM((tok, kv), f32),
            pltpu.VMEM((tok, LANES), f32),
            pltpu.VMEM((tok, LANES), f32),
            pltpu.VMEM((tok, LANES), jnp.int32),
            pltpu.VMEM((KVH, rows, nq, HD), bf16),
            pltpu.VMEM((KVH, rows, nq, HD), bf16),
            pltpu.VMEM((KVH, blocks, 2, LANES), f32),
            pltpu.VMEM((n, nq, HD), bf16),
            pltpu.VMEM((n, 2, LANES), f32),
            pltpu.VMEM((16, HD), bf16),
            pltpu.VMEM((16, HD), bf16),
            pltpu.VMEM((LANES, LANES), f32),
            pltpu.SemaphoreType.DMA((chunks,)),
            pltpu.SemaphoreType.DMA((chunks,)),
            pltpu.SemaphoreType.DMA((chunks,)),
            pltpu.SemaphoreType.DMA((n,)),
            pltpu.SemaphoreType.DMA((n,)),
            pltpu.SemaphoreType.DMA((n,)),
            pltpu.SemaphoreType.DMA((n,)),
            pltpu.SemaphoreType.DMA((n,)),
            pltpu.SemaphoreType.DMA((n,)),
        ],
        compiler_params=pltpu.CompilerParams(
            collective_id=0, has_side_effects=True, vmem_limit_bytes=40 * 1024 * 1024
        ),
    )(
        lengths,
        dest_rows,
        hidden,
        key_weight,
        value_weight,
        key_gain[None, :],
        freq,
        queries,
        new_keys,
        new_values,
    )


def solution(mesh):
    placed = (
        P(("groups", "ctx"), None),
        P(),
        P(),
        P(),
        P("groups"),
        P("groups"),
        P(("groups", "ctx"), None, None),
        P(("groups", "ctx"), None, None),
        P(("groups", "ctx"), None, None),
    )
    return jax.shard_map(
        local,
        mesh=mesh,
        in_specs=placed,
        out_specs=P(("groups", "ctx"), None, None),
        check_vma=False,
    )
```

time: 130 us -> 37.7 us (0.29)
  the two profiles are of different devices: /device:TPU:0 before, /device:TPU:3 now
where the time goes in v1:
time: 37.7 us; the launch traced here: 37.4 us
  Pallas kernels  25.3 us (67%)
  local copies, waits for them, and re-layouts  12.1 us (32%)
    pallas_call x1, Pallas kernels, local(): pl.pallas_call(functools.partial(kernel, n, rows), out_shape=jax.ShapeDty...  25.3 us
    unnamed x21, local copies, waits for them, and re-layouts  12.1 us

profile of v1, /device:TPU:3, one launch (start us, length us, event | category | flops | bytes accessed | tf_op | source)
XLA Modules:
  0.0 37.4 jit_solution(4939991028774097191)
XLA Ops:
  0.0 0.0 copy-start
  0.0 2.5 %copy-done = bf16[5120,512]{1,0:T(8,128)(2,1)S(1)} copy-done((bf16[5120,512]{1,0:T(8,128)(2,1)S(1)}, bf16[5120,512]{1,0:T(8,128)(2,1)}, u32[]{:S(2)}) %copy-start) | copy-done | bytes 5242904
  2.5 0.0 copy-start.1
  2.5 2.5 %copy-done.1 = bf16[5120,512]{1,0:T(8,128)(2,1)S(1)} copy-done((bf16[5120,512]{1,0:T(8,128)(2,1)S(1)}, bf16[5120,512]{1,0:T(8,128)(2,1)}, u32[]{:S(2)}) %copy-start.1) | copy-done | bytes 5242904
  5.0 0.0 copy-start.2
  5.0 1.8 %copy-done.2 = bf16[288,5120]{1,0:T(8,128)(2,1)S(1)} copy-done((bf16[288,5120]{1,0:T(8,128)(2,1)S(1)}, bf16[288,5120]{1,0:T(8,128)(2,1)}, u32[]{:S(2)}) %copy-start.2) | copy-done | bytes 2949144
  6.8 0.0 copy-start.3
  6.8 0.7 %copy-done.3 = bf16[1,32,128]{2,1,0:T(8,128)(2,1)S(1)} copy-done((bf16[1,32,128]{2,1,0:T(8,128)(2,1)S(1)}, bf16[1,32,128]{2,1,0:T(8,128)(2,1)}, u32[]{:S(2)}) %copy-start.3) | copy-done | bytes 8216
  7.5 0.0 copy-start.4
  7.5 0.7 %copy-done.4 = bf16[1,4,128]{2,1,0:T(4,128)(2,1)S(1)} copy-done((bf16[1,4,128]{2,1,0:T(4,128)(2,1)S(1)}, bf16[1,4,128]{2,1,0:T(4,128)(2,1)}, u32[]{:S(2)}) %copy-start.4) | copy-done | bytes 1048
  8.2 0.0 copy-start.5
  8.2 0.7 %copy-done.5 = bf16[1,4,128]{2,1,0:T(4,128)(2,1)S(1)} copy-done((bf16[1,4,128]{2,1,0:T(4,128)(2,1)S(1)}, bf16[1,4,128]{2,1,0:T(4,128)(2,1)}, u32[]{:S(2)}) %copy-start.5) | copy-done | bytes 1048
  8.9 0.0 copy-start.6
  8.9 0.7 %copy-done.6 = s32[8]{0:T(128)S(1)} copy-done((s32[8]{0:T(128)S(1)}, s32[8]{0:T(128)}, u32[]{:S(2)}) %copy-start.6) | copy-done | bytes 56
  9.5 0.0 copy-start.7
  9.5 0.7 %copy-done.7 = s32[8]{0:T(128)S(1)} copy-done((s32[8]{0:T(128)S(1)}, s32[8]{0:T(128)}, u32[]{:S(2)}) %copy-start.7) | copy-done | bytes 56
  10.2 0.0 copy-start.8
  10.2 0.7 %copy-done.8 = f32[128]{0:T(128)S(1)} copy-done((f32[128]{0:T(128)S(1)}, f32[128]{0:T(128)}, u32[]{:S(2)}) %copy-start.8) | copy-done | bytes 536
  10.8 0.0 copy-start.9
  10.8 0.7 %copy-done.9 = f32[1,128]{1,0:T(1,128)S(1)} copy-done((f32[1,128]{1,0:T(1,128)S(1)}, f32[1,128]{1,0:T(1,128)}, u32[]{:S(2)}) %copy-start.9) | copy-done | bytes 536
  11.5 25.3 %shard_map.100 = bf16[1,32,128]{2,1,0:T(8,128)(2,1)S(1)} custom-call(s32[8]{0:T(128)S(1)} %copy-done.6, s32[8]{0:T(128)S(1)} %copy-done.7, bf16[288,5120]{1,0:T(8,128)(2,1)S(1)} %copy-done.2, bf16[5120,512]{1,0:T(8,128)(2,1)S(1)} %copy-done, bf16[5120,512]{1,0:T(8,128)(2,1)S(1)} %copy-done.1, f32[1,128]{1,0:T(1,128)S(1)} %bitcast.1, f32[1,128]{1,0:T(1,128)S(1)} %copy-done.9, ...), custom_call_target="tpu_custom_call" | custom-call | tf_op jit(solution)/shard_map/pallas_call | solution.py:280
  36.8 0.6 %copy.12 = bf16[1,32,128]{2,1,0:T(8,128)(2,1)} copy(bf16[1,32,128]{2,1,0:T(8,128)(2,1)S(1)} %shard_map.100) | data formatting | bytes 16384
Async XLA Ops:
  0.0 2.5 %copy-start = (bf16[5120,512]{1,0:T(8,128)(2,1)S(1)}, bf16[5120,512]{1,0:T(8,128)(2,1)}, u32[]{:S(2)}) copy-start(bf16[5120,512]{1,0:T(8,128)(2,1)} %key_weight.1) | copy-start | bytes 15728644
  2.5 2.5 %copy-start.1 = (bf16[5120,512]{1,0:T(8,128)(2,1)S(1)}, bf16[5120,512]{1,0:T(8,128)(2,1)}, u32[]{:S(2)}) copy-start(bf16[5120,512]{1,0:T(8,128)(2,1)} %value_weight.1) | copy-start | bytes 15728644
  5.0 1.8 %copy-start.2 = (bf16[288,5120]{1,0:T(8,128)(2,1)S(1)}, bf16[288,5120]{1,0:T(8,128)(2,1)}, u32[]{:S(2)}) copy-start(bf16[288,5120]{1,0:T(8,128)(2,1)} %hidden.1) | copy-start | bytes 8847364
  6.8 0.7 %copy-start.3 = (bf16[1,32,128]{2,1,0:T(8,128)(2,1)S(1)}, bf16[1,32,128]{2,1,0:T(8,128)(2,1)}, u32[]{:S(2)}) copy-start(bf16[1,32,128]{2,1,0:T(8,128)(2,1)} %query.1) | copy-start | bytes 24580
  7.5 0.7 %copy-start.4 = (bf16[1,4,128]{2,1,0:T(4,128)(2,1)S(1)}, bf16[1,4,128]{2,1,0:T(4,128)(2,1)}, u32[]{:S(2)}) copy-start(bf16[1,4,128]{2,1,0:T(4,128)(2,1)} %new_keys.1) | copy-start | bytes 3076
  8.2 0.7 %copy-start.5 = (bf16[1,4,128]{2,1,0:T(4,128)(2,1)S(1)}, bf16[1,4,128]{2,1,0:T(4,128)(2,1)}, u32[]{:S(2)}) copy-start(bf16[1,4,128]{2,1,0:T(4,128)(2,1)} %new_values.1) | copy-start | bytes 3076
  8.9 0.7 %copy-start.6 = (s32[8]{0:T(128)S(1)}, s32[8]{0:T(128)}, u32[]{:S(2)}) copy-start(s32[8]{0:T(128)} %lengths.1) | copy-start | bytes 100
  9.5 0.7 %copy-start.7 = (s32[8]{0:T(128)S(1)}, s32[8]{0:T(128)}, u32[]{:S(2)}) copy-start(s32[8]{0:T(128)} %dest_rows.1) | copy-start | bytes 100
  10.2 0.7 %copy-start.8 = (f32[128]{0:T(128)S(1)}, f32[128]{0:T(128)}, u32[]{:S(2)}) copy-start(f32[128]{0:T(128)} %param.13) | copy-start | bytes 1540
  10.8 0.7 %copy-start.9 = (f32[1,128]{1,0:T(1,128)S(1)}, f32[1,128]{1,0:T(1,128)}, u32[]{:S(2)}) copy-start(f32[1,128]{1,0:T(1,128)} %constant.2.clone.freq) | copy-start | bytes 1540

commit v2 on v1

v2 whole, which is shorter than its diff:
```python
import functools

import jax
import jax.numpy as jnp
import numpy as np
from jax import lax
from jax.experimental import pallas as pl
from jax.experimental.pallas import tpu as pltpu
from jax.sharding import PartitionSpec as P

KVH = 4
HD = 128
QPK = 8
HALF = KVH // 2
LANES = 128

ROPE_BASE = 1000000.0
EPS = 1e-06
NEG = -1e30
MESH = pl.DeviceIdType.MESH
CONTRACT_LAST = (((1,), (1,)), ((), ()))
CONTRACT_FIRST = (((0,), (0,)), ((), ()))


def kernel(
    n,
    rows,
    early,
    lengths_hbm,
    dest_hbm,
    hidden,
    key_weight,
    value_weight,
    gain_hbm,
    freq_hbm,
    query_hbm,
    new_keys_hbm,
    new_values_hbm,
    out,
    lengths,
    dest_rows,
    gain,
    freq,
    query,
    new_keys,
    new_values,
    hid_v,
    kw_v,
    vw_v,
    acc_k,
    acc_v,
    cos_v,
    sin_v,
    row_v,
    qbuf,
    k_send,
    v_send,
    k_all,
    v_all,
    o_send,
    s_send,
    o_recv,
    s_recv,
    near_k,
    near_v,
    mix_v,
    small_sem,
    hid_sem,
    kw_sem,
    vw_sem,
    q_send_sem,
    q_recv_sem,
    kv_send_sem,
    kv_recv_sem,
    o_send_sem,
    o_recv_sem,
    s_send_sem,
    s_recv_sem,
):
    me = lax.axis_index("ctx")
    core, chip = lax.rem(me, 2), me // 2
    sibling = me + 1 - 2 * core
    chips = n // 2
    my_row, my_k = chip // HALF, lax.rem(chip, HALF)
    chunks, tok, depth = hid_v.shape
    nq = query.shape[1]
    scale = 1.0 / HD**0.5
    wide = rows * nq

    def chunk_copies(c):
        part = pl.ds(pl.multiple_of(c * depth, depth), depth)
        return (
            pltpu.make_async_copy(hidden.at[:, part], hid_v.at[c], hid_sem.at[c]),
            pltpu.make_async_copy(key_weight.at[part], kw_v.at[c], kw_sem.at[c]),
            pltpu.make_async_copy(value_weight.at[part], vw_v.at[c], vw_sem.at[c]),
        )

    def remote(src, dst, send_sem, recv_sem, device):
        return pltpu.make_async_remote_copy(
            src_ref=src,
            dst_ref=dst,
            send_sem=send_sem,
            recv_sem=recv_sem,
            device_id={"ctx": device},
            device_id_type=MESH,
        )

    def query_copy(other, source):
        slot = qbuf.at[lax.rem(source, HALF), source // HALF]
        return remote(
            qbuf.at[my_k, my_row],
            slot,
            q_send_sem.at[other],
            q_recv_sem.at[source],
            other * 2 + core,
        )

    def part_copies(k, r, source):
        other = r * HALF + k
        device = other * 2 + core
        return (
            remote(
                o_send.at[k, r],
                o_recv.at[source],
                o_send_sem.at[other],
                o_recv_sem.at[source],
                device,
            ),
            remote(
                s_send.at[k, r * nq // LANES],
                s_recv.at[source],
                s_send_sem.at[other],
                s_recv_sem.at[source],
                device,
            ),
        )

    key_copies = [
        remote(k_send.at[k], k_all.at[k, 1], kv_send_sem.at[k], kv_recv_sem.at[k], sibling)
        for k in range(HALF)
    ]
    value_copies = [
        remote(
            v_send.at[k],
            v_all.at[k, 1],
            kv_send_sem.at[HALF + k],
            kv_recv_sem.at[HALF + k],
            sibling,
        )
        for k in range(HALF)
    ]

    small = [
        pltpu.make_async_copy(src, dst, small_sem.at[i])
        for i, (src, dst) in enumerate(
            [
                (lengths_hbm, lengths),
                (dest_hbm, dest_rows),
                (freq_hbm, freq),
                (query_hbm, query),
                (gain_hbm, gain),
                (new_keys_hbm, new_keys),
                (new_values_hbm, new_values),
            ]
        )
    ]
    for copy in small:
        copy.start()

    barrier = pltpu.get_barrier_semaphore()

    @pl.loop(1, chips)
    def _(i):
        pl.semaphore_signal(
            barrier,
            inc=1,
            device_id={"ctx": lax.rem(chip + i, chips) * 2 + core},
            device_id_type=MESH,
        )

    pl.semaphore_signal(barrier, inc=1, device_id={"ctx": sibling}, device_id_type=MESH)

    @pl.loop(0, chunks)
    def _(c):
        for copy in chunk_copies(c):
            copy.start()

    for copy in small:
        copy.wait()
    qbuf[my_k, my_row] = query[0]

    count = lax.broadcasted_iota(jnp.int32, (tok, LANES), 0)
    lane = lax.broadcasted_iota(jnp.int32, (tok, LANES), 1)
    for side, device in enumerate((me, sibling)):
        stream = device * tok + count
        begin = jnp.int32(0)
        start_of = jnp.zeros((tok, LANES), jnp.int32)
        row_of = jnp.zeros((tok, LANES), jnp.int32)
        for p in range(rows):
            inside = stream >= begin
            if side == 0:
                start_of = jnp.where(inside, begin, start_of)
            row_of = jnp.where(inside, dest_rows[p], row_of)
            begin = begin + lengths[p]
        row_v[side] = row_of
        if side == 0:
            angle = (stream - start_of).astype(jnp.float32) * freq[...]
            cos_v[...] = jnp.cos(angle)
            sine = jnp.sin(angle)
            sin_v[...] = jnp.where(lane < HD // 2, -sine, sine)

    steps = new_keys.shape[1]
    near_k[...] = jnp.zeros_like(near_k)
    near_v[...] = jnp.zeros_like(near_v)
    near_k[0:steps] = new_keys[0]
    near_v[0:steps] = new_values[0]
    own = jnp.concatenate([query[0]] * (LANES // nq), 0)
    near = lax.dot_general(near_k[...], own, CONTRACT_LAST, preferred_element_type=jnp.float32)
    near = near * scale
    u = lax.broadcasted_iota(jnp.int32, near.shape, 0)
    step_of = lax.broadcasted_iota(jnp.int32, near.shape, 1) % nq // QPK
    allowed = u <= jnp.minimum(step_of, steps - 1)
    near = jnp.where(allowed, near, NEG)
    near_top = jnp.max(near, 0, keepdims=True)
    near_w = jnp.where(allowed, jnp.exp(near - near_top), 0.0)
    near_sum = jnp.sum(near_w, 0, keepdims=True)
    near_o = lax.dot_general(
        near_w.astype(jnp.bfloat16), near_v[...], CONTRACT_FIRST, preferred_element_type=jnp.float32
    )[:nq]

    acc_k[...] = jnp.zeros_like(acc_k)
    acc_v[...] = jnp.zeros_like(acc_v)

    def project(c):
        for copy in chunk_copies(c):
            copy.wait()
        h = hid_v[c]
        acc_k[...] += jnp.dot(h, kw_v[c], preferred_element_type=jnp.float32)
        acc_v[...] += jnp.dot(h, vw_v[c], preferred_element_type=jnp.float32)

    pl.loop(0, early)(project)
    pl.semaphore_wait(barrier, chips)

    @pl.loop(1, chips)
    def _(i):
        query_copy(lax.rem(chip + i, chips), chip).start()

    pl.loop(early, chunks)(project)

    def columns(k, side):
        head = 2 * k + (core if side == 0 else 1 - core)
        return pl.ds(pl.multiple_of(head * HD, HD), HD)

    def make_keys(k, side):
        raw = acc_k[:, columns(k, side)]
        normed = raw * lax.rsqrt(jnp.mean(raw * raw, -1, keepdims=True) + EPS) * gain[...]
        keys = normed * cos_v[...] + pltpu.roll(normed, HD // 2, 1) * sin_v[...]
        return keys.astype(jnp.bfloat16)

    for k in range(HALF):
        k_send[k] = make_keys(k, 1)
        key_copies[k].start()
    for k in range(HALF):
        v_send[k] = acc_v[:, columns(k, 1)].astype(jnp.bfloat16)
        value_copies[k].start()
    for k in range(HALF):
        k_all[k, 0] = make_keys(k, 0)
        v_all[k, 0] = acc_v[:, columns(k, 0)].astype(jnp.bfloat16)

    @pl.loop(1, chips)
    def _(i):
        other = lax.rem(chip + i, chips)
        query_copy(other, other).wait_recv()

    column_row = lax.broadcasted_iota(jnp.int32, (2 * tok, wide), 1) // nq
    row_of = jnp.concatenate([row_v[...].reshape(2 * tok, LANES)] * (wide // LANES), 1)
    live = row_of == column_row
    for k in range(HALF):
        key_copies[k].wait_recv()
        far = lax.dot_general(
            k_all[k].reshape(2 * tok, HD),
            qbuf[k].reshape(wide, HD),
            CONTRACT_LAST,
            preferred_element_type=jnp.float32,
        )
        far = jnp.where(live, far * scale, NEG)
        top = jnp.max(far, 0, keepdims=True)
        weights = jnp.where(live, jnp.exp(far - top), 0.0)
        total = jnp.sum(weights, 0, keepdims=True)
        value_copies[k].wait_recv()
        mixed = lax.dot_general(
            weights.astype(jnp.bfloat16),
            v_all[k].reshape(2 * tok, HD),
            CONTRACT_FIRST,
            preferred_element_type=jnp.float32,
        )
        o_send[k] = mixed.astype(jnp.bfloat16).reshape(rows, nq, HD)
        for b in range(wide // LANES):
            block = slice(b * LANES, (b + 1) * LANES)
            s_send[k, b] = jnp.concatenate([top[:, block], total[:, block]], 0)

        @pl.loop(0, rows)
        def _(i):
            r = lax.rem(my_row + i, rows)

            @pl.when(r * HALF + k != chip)
            def _():
                for copy in part_copies(k, r, chip):
                    copy.start()

    o_recv[chip] = o_send[my_k, my_row]
    s_recv[chip] = s_send[my_k, my_row * nq // LANES]

    @pl.loop(1, chips)
    def _(i):
        other = lax.rem(chip + i, chips)
        for copy in part_copies(lax.rem(other, HALF), other // HALF, other):
            copy.wait_recv()

    tops, sums = s_recv[:, 0, :], s_recv[:, 1, :]
    best = jnp.maximum(jnp.max(tops, 0, keepdims=True), near_top)
    factor = jnp.exp(tops - best)
    near_factor = jnp.exp(near_top - best)
    total = jnp.sum(factor * sums, 0, keepdims=True) + near_factor * near_sum
    shares = jnp.concatenate(
        [
            factor / total,
            near_factor / total,
            jnp.zeros((LANES - chips - 1, LANES), jnp.float32),
        ],
        0,
    )
    mix_v[...] = shares.T
    mine = mix_v[pl.ds(pl.multiple_of(lax.rem(my_row * nq, LANES), nq), nq), :]
    result = near_o * mine[:, chips : chips + 1]
    for s in range(chips):
        result = result + o_recv[s].astype(jnp.float32) * mine[:, s : s + 1]
    out[0] = result.astype(jnp.bfloat16)

    for copy in key_copies + value_copies:
        copy.wait_send()

    @pl.loop(1, chips)
    def _(i):
        other = lax.rem(chip + i, chips)
        query_copy(other, chip).wait_send()
        for copy in part_copies(lax.rem(other, HALF), other // HALF, chip):
            copy.wait_send()


def local(
    hidden, key_weight, value_weight, key_gain, lengths, dest_rows, queries, new_keys, new_values
):
    n = lax.axis_size("ctx")
    chips = n // 2
    rows = lengths.shape[0]
    tok, width = hidden.shape
    nq = queries.shape[1]
    kv = KVH * HD
    depth = 512
    chunks = width // depth
    half = np.arange(HD // 2, dtype=np.float32)
    freq = np.power(np.float32(ROPE_BASE), np.float32(-2.0) * half / np.float32(HD))
    freq = jnp.asarray(np.concatenate([freq, freq])[None, :].astype(np.float32))
    vmem = pl.BlockSpec(memory_space=pltpu.VMEM)
    hbm = pl.BlockSpec(memory_space=pltpu.HBM)
    bf16, f32 = jnp.bfloat16, jnp.float32
    blocks = rows * nq // LANES
    return pl.pallas_call(
        functools.partial(kernel, n, rows, chunks // 2),
        out_shape=jax.ShapeDtypeStruct((1, nq, HD), bf16),
        in_specs=[hbm] * 10,
        out_specs=vmem,
        scratch_shapes=[
            pltpu.SMEM((rows,), jnp.int32),
            pltpu.SMEM((rows,), jnp.int32),
            pltpu.VMEM((1, HD), f32),
            pltpu.VMEM((1, LANES), f32),
            pltpu.VMEM((1, nq, HD), bf16),
            pltpu.VMEM(new_keys.shape, bf16),
            pltpu.VMEM(new_values.shape, bf16),
            pltpu.VMEM((chunks, tok, depth), bf16),
            pltpu.VMEM((chunks, depth, kv), bf16),
            pltpu.VMEM((chunks, depth, kv), bf16),
            pltpu.VMEM((tok, kv), f32),
            pltpu.VMEM((tok, kv), f32),
            pltpu.VMEM((tok, LANES), f32),
            pltpu.VMEM((tok, LANES), f32),
            pltpu.VMEM((2, tok, LANES), jnp.int32),
            pltpu.VMEM((HALF, rows, nq, HD), bf16),
            pltpu.VMEM((HALF, tok, HD), bf16),
            pltpu.VMEM((HALF, tok, HD), bf16),
            pltpu.VMEM((HALF, 2, tok, HD), bf16),
            pltpu.VMEM((HALF, 2, tok, HD), bf16),
            pltpu.VMEM((HALF, rows, nq, HD), bf16),
            pltpu.VMEM((HALF, blocks, 2, LANES), f32),
            pltpu.VMEM((chips, nq, HD), bf16),
            pltpu.VMEM((chips, 2, LANES), f32),
            pltpu.VMEM((16, HD), bf16),
            pltpu.VMEM((16, HD), bf16),
            pltpu.VMEM((LANES, LANES), f32),
            pltpu.SemaphoreType.DMA((7,)),
            pltpu.SemaphoreType.DMA((chunks,)),
            pltpu.SemaphoreType.DMA((chunks,)),
            pltpu.SemaphoreType.DMA((chunks,)),
            pltpu.SemaphoreType.DMA((chips,)),
            pltpu.SemaphoreType.DMA((chips,)),
            pltpu.SemaphoreType.DMA((KVH,)),
            pltpu.SemaphoreType.DMA((KVH,)),
            pltpu.SemaphoreType.DMA((chips,)),
            pltpu.SemaphoreType.DMA((chips,)),
            pltpu.SemaphoreType.DMA((chips,)),
            pltpu.SemaphoreType.DMA((chips,)),
        ],
        compiler_params=pltpu.CompilerParams(
            collective_id=0, has_side_effects=True, vmem_limit_bytes=60 * 1024 * 1024
        ),
    )(
        lengths,
        dest_rows,
        hidden,
        key_weight,
        value_weight,
        key_gain[None, :],
        freq,
        queries,
        new_keys,
        new_values,
    )


def solution(mesh):
    placed = (
        P(("groups", "ctx"), None),
        P(),
        P(),
        P(),
        P("groups"),
        P("groups"),
        P(("groups", "ctx"), None, None),
        P(("groups", "ctx"), None, None),
        P(("groups", "ctx"), None, None),
    )
    return jax.shard_map(
        local,
        mesh=mesh,
        in_specs=placed,
        out_specs=P(("groups", "ctx"), None, None),
        check_vma=False,
    )
```

time: 37.7 us -> 21.9 us (0.58)
  the two profiles are of different devices: /device:TPU:3 before, /device:TPU:0 now
where the time goes in v2:
time: 21.9 us; the launch traced here: 21.7 us
  Pallas kernels  20.4 us (93%)
  local copies, waits for them, and re-layouts  1.3 us (6%)
    pallas_call x1, Pallas kernels, local(): pl.pallas_call(functools.partial(kernel, n, rows, chunks // 2), out_shape...  20.4 us
    unnamed x1, local copies, waits for them, and re-layouts  1.3 us

profile of v2, /device:TPU:0, one launch (start us, length us, event | category | flops | bytes accessed | tf_op | source)
XLA Modules:
  0.0 21.7 jit_solution(9970962834884309533)
XLA Ops:
  0.0 20.4 %shard_map.100 = bf16[1,32,128]{2,1,0:T(8,128)(2,1)} custom-call(s32[8]{0:T(128)} %lengths_hbm.1, s32[8]{0:T(128)} %dest_hbm.1, bf16[288,5120]{1,0:T(8,128)(2,1)} %hidden.1, bf16[5120,512]{1,0:T(8,128)(2,1)} %key_weight.1, bf16[5120,512]{1,0:T(8,128)(2,1)} %value_weight.1, f32[1,128]{1,0:T(1,128)} %bitcast.1, f32[1,128]{1,0:T(1,128)} %constant.2.clone.freq_hbm, ...), custom_call_target="tpu_custom_call" | custom-call | tf_op jit(solution)/shard_map/pallas_call | solution.py:369
  20.4 1.3 %copy.12 = bf16[1,32,128]{2,1,0:T(8,128)(2,1)} copy(bf16[1,32,128]{2,1,0:T(8,128)(2,1)} %shard_map.100) | data formatting | bytes 16384

commit v3 on v2

--- a/solution.py
+++ b/solution.py
@@ -26,6 +26,7 @@
     n,
     rows,
     early,
+    ahead,
     lengths_hbm,
     dest_hbm,
     hidden,
@@ -164,9 +165,6 @@
             ]
         )
     ]
-    for copy in small:
-        copy.start()
-
     barrier = pltpu.get_barrier_semaphore()
 
     @pl.loop(1, chips)
@@ -180,7 +178,10 @@
 
     pl.semaphore_signal(barrier, inc=1, device_id={"ctx": sibling}, device_id_type=MESH)
 
-    @pl.loop(0, chunks)
+    for copy in small:
+        copy.start()
+
+    @pl.loop(0, min(ahead, chunks))
     def _(c):
         for copy in chunk_copies(c):
             copy.start()
@@ -189,25 +190,117 @@
         copy.wait()
     qbuf[my_k, my_row] = query[0]
 
-    count = lax.broadcasted_iota(jnp.int32, (tok, LANES), 0)
-    lane = lax.broadcasted_iota(jnp.int32, (tok, LANES), 1)
-    for side, device in enumerate((me, sibling)):
-        stream = device * tok + count
+    span = min(-(-tok // (8 * chunks)) * 8, tok)
+    count = lax.broadcasted_iota(jnp.int32, (span, LANES), 0)
+    lane = lax.broadcasted_iota(jnp.int32, (span, LANES), 1)
+
+    def tables(c):
+        first = pl.multiple_of(jnp.minimum(c * span, tok - span), 8)
+        place = pl.ds(first, span)
+        mine, theirs = (device * tok + first + count for device in (me, sibling))
         begin = jnp.int32(0)
-        start_of = jnp.zeros((tok, LANES), jnp.int32)
-        row_of = jnp.zeros((tok, LANES), jnp.int32)
+        start_of = jnp.zeros((span, LANES), jnp.int32)
+        my_rows = jnp.zeros((span, LANES), jnp.int32)
+        their_rows = jnp.zeros((span, LANES), jnp.int32)
         for p in range(rows):
-            inside = stream >= begin
-            if side == 0:
-                start_of = jnp.where(inside, begin, start_of)
-            row_of = jnp.where(inside, dest_rows[p], row_of)
+            inside = mine >= begin
+            start_of = jnp.where(inside, begin, start_of)
+            my_rows = jnp.where(inside, dest_rows[p], my_rows)
+            their_rows = jnp.where(theirs >= begin, dest_rows[p], their_rows)
             begin = begin + lengths[p]
-        row_v[side] = row_of
-        if side == 0:
-            angle = (stream - start_of).astype(jnp.float32) * freq[...]
-            cos_v[...] = jnp.cos(angle)
-            sine = jnp.sin(angle)
-            sin_v[...] = jnp.where(lane < HD // 2, -sine, sine)
+        row_v[0, place] = my_rows
+        row_v[1, place] = their_rows
+        angle = (mine - start_of).astype(jnp.float32) * freq[...]
+        cos_v[place] = jnp.cos(angle)
+        sine = jnp.sin(angle)
+        sin_v[place] = jnp.where(lane < HD // 2, -sine, sine)
+
+    acc_k[...] = jnp.zeros_like(acc_k)
+    acc_v[...] = jnp.zeros_like(acc_v)
+
+    def project(c):
+        for copy in chunk_copies(c):
+            copy.wait()
+
+        @pl.when(c + ahead < chunks)
+        def _():
+            for copy in chunk_copies(c + ahead):
+                copy.start()
+
+        tables(c)
+        h = hid_v[c]
+        acc_k[...] += jnp.dot(h, kw_v[c], preferred_element_type=jnp.float32)
+        acc_v[...] += jnp.dot(h, vw_v[c], preferred_element_type=jnp.float32)
+
+    pl.loop(0, early)(project)
+    pl.semaphore_wait(barrier, chips)
+
+    @pl.loop(1, chips)
+    def _(i):
+        query_copy(lax.rem(chip + i, chips), chip).start()
+
+    pl.loop(early, chunks)(project)
+
+    def columns(k, side):
+        head = 2 * k + (core if side == 0 else 1 - core)
+        return pl.ds(pl.multiple_of(head * HD, HD), HD)
+
+    def make_keys(k, side):
+        raw = acc_k[:, columns(k, side)]
+        normed = raw * lax.rsqrt(jnp.mean(raw * raw, -1, keepdims=True) + EPS) * gain[...]
+        keys = normed * cos_v[...] + pltpu.roll(normed, HD // 2, 1) * sin_v[...]
+        return keys.astype(jnp.bfloat16)
+
+    for k in range(HALF):
+        k_send[k] = make_keys(k, 1)
+        key_copies[k].start()
+    for k in range(HALF):
+        v_send[k] = acc_v[:, columns(k, 1)].astype(jnp.bfloat16)
+        value_copies[k].start()
+    for k in range(HALF):
+        k_all[k, 0] = make_keys(k, 0)
+        v_all[k, 0] = acc_v[:, columns(k, 0)].astype(jnp.bfloat16)
+
+    @pl.loop(1, chips)
+    def _(i):
+        other = lax.rem(chip + i, chips)
+        query_copy(other, other).wait_recv()
+
+    column_row = lax.broadcasted_iota(jnp.int32, (2 * tok, wide), 1) // nq
+    row_of = jnp.concatenate([row_v[...].reshape(2 * tok, LANES)] * (wide // LANES), 1)
+    live = row_of == column_row
+    for k in range(HALF):
+        key_copies[k].wait_recv()
+        far = lax.dot_general(
+            k_all[k].reshape(2 * tok, HD),
+            qbuf[k].reshape(wide, HD),
+            CONTRACT_LAST,
+            preferred_element_type=jnp.float32,
+        )
+        far = jnp.where(live, far * scale, NEG)
+        top = jnp.max(far, 0, keepdims=True)
+        weights = jnp.where(live, jnp.exp(far - top), 0.0)
+        total = jnp.sum(weights, 0, keepdims=True)
+        value_copies[k].wait_recv()
+        mixed = lax.dot_general(
+            weights.astype(jnp.bfloat16),
+            v_all[k].reshape(2 * tok, HD),
+            CONTRACT_FIRST,
+            preferred_element_type=jnp.float32,
+        )
+        o_send[k] = mixed.astype(jnp.bfloat16).reshape(rows, nq, HD)
+        for b in range(wide // LANES):
+            block = slice(b * LANES, (b + 1) * LANES)
+            s_send[k, b] = jnp.concatenate([top[:, block], total[:, block]], 0)
+
+        @pl.loop(0, rows)
+        def _(i):
+            r = lax.rem(my_row + i, rows)
+
+            @pl.when(r * HALF + k != chip)
+            def _():
+                for copy in part_copies(k, r, chip):
+                    copy.start()
 
     steps = new_keys.shape[1]
     near_k[...] = jnp.zeros_like(near_k)
@@ -228,88 +321,18 @@
         near_w.astype(jnp.bfloat16), near_v[...], CONTRACT_FIRST, preferred_element_type=jnp.float32
     )[:nq]
 
-    acc_k[...] = jnp.zeros_like(acc_k)
-    acc_v[...] = jnp.zeros_like(acc_v)
-
-    def project(c):
-        for copy in chunk_copies(c):
-            copy.wait()
-        h = hid_v[c]
-        acc_k[...] += jnp.dot(h, kw_v[c], preferred_element_type=jnp.float32)
-        acc_v[...] += jnp.dot(h, vw_v[c], preferred_element_type=jnp.float32)
-
-    pl.loop(0, early)(project)
-    pl.semaphore_wait(barrier, chips)
-
-    @pl.loop(1, chips)
-    def _(i):
-        query_copy(lax.rem(chip + i, chips), chip).start()
-
-    pl.loop(early, chunks)(project)
-
-    def columns(k, side):
-        head = 2 * k + (core if side == 0 else 1 - core)
-        return pl.ds(pl.multiple_of(head * HD, HD), HD)
-
-    def make_keys(k, side):
-        raw = acc_k[:, columns(k, side)]
-        normed = raw * lax.rsqrt(jnp.mean(raw * raw, -1, keepdims=True) + EPS) * gain[...]
-        keys = normed * cos_v[...] + pltpu.roll(normed, HD // 2, 1) * sin_v[...]
-        return keys.astype(jnp.bfloat16)
-
-    for k in range(HALF):
-        k_send[k] = make_keys(k, 1)
-        key_copies[k].start()
-    for k in range(HALF):
-        v_send[k] = acc_v[:, columns(k, 1)].astype(jnp.bfloat16)
-        value_copies[k].start()
-    for k in range(HALF):
-        k_all[k, 0] = make_keys(k, 0)
-        v_all[k, 0] = acc_v[:, columns(k, 0)].astype(jnp.bfloat16)
+    o_recv[chip] = o_send[my_k, my_row]
+    s_recv[chip] = s_send[my_k, my_row * nq // LANES]
+
+    for copy in key_copies + value_copies:
+        copy.wait_send()
 
     @pl.loop(1, chips)
     def _(i):
         other = lax.rem(chip + i, chips)
-        query_copy(other, other).wait_recv()
-
-    column_row = lax.broadcasted_iota(jnp.int32, (2 * tok, wide), 1) // nq
-    row_of = jnp.concatenate([row_v[...].reshape(2 * tok, LANES)] * (wide // LANES), 1)
-    live = row_of == column_row
-    for k in range(HALF):
-        key_copies[k].wait_recv()
-        far = lax.dot_general(
-            k_all[k].reshape(2 * tok, HD),
-            qbuf[k].reshape(wide, HD),
-            CONTRACT_LAST,
-            preferred_element_type=jnp.float32,
-        )
-        far = jnp.where(live, far * scale, NEG)
-        top = jnp.max(far, 0, keepdims=True)
-        weights = jnp.where(live, jnp.exp(far - top), 0.0)
-        total = jnp.sum(weights, 0, keepdims=True)
-        value_copies[k].wait_recv()
-        mixed = lax.dot_general(
-            weights.astype(jnp.bfloat16),
-            v_all[k].reshape(2 * tok, HD),
-            CONTRACT_FIRST,
-            preferred_element_type=jnp.float32,
-        )
-        o_send[k] = mixed.astype(jnp.bfloat16).reshape(rows, nq, HD)
-        for b in range(wide // LANES):
-            block = slice(b * LANES, (b + 1) * LANES)
-            s_send[k, b] = jnp.concatenate([top[:, block], total[:, block]], 0)
-
-        @pl.loop(0, rows)
-        def _(i):
-            r = lax.rem(my_row + i, rows)
-
-            @pl.when(r * HALF + k != chip)
-            def _():
-                for copy in part_copies(k, r, chip):
-                    copy.start()
-
-    o_recv[chip] = o_send[my_k, my_row]
-    s_recv[chip] = s_send[my_k, my_row * nq // LANES]
+        query_copy(other, chip).wait_send()
+        for copy in part_copies(lax.rem(other, HALF), other // HALF, chip):
+            copy.wait_send()
 
     @pl.loop(1, chips)
     def _(i):
@@ -337,16 +360,6 @@
         result = result + o_recv[s].astype(jnp.float32) * mine[:, s : s + 1]
     out[0] = result.astype(jnp.bfloat16)
 
-    for copy in key_copies + value_copies:
-        copy.wait_send()
-
-    @pl.loop(1, chips)
-    def _(i):
-        other = lax.rem(chip + i, chips)
-        query_copy(other, chip).wait_send()
-        for copy in part_copies(lax.rem(other, HALF), other // HALF, chip):
-            copy.wait_send()
-
 
 def local(
     hidden, key_weight, value_weight, key_gain, lengths, dest_rows, queries, new_keys, new_values
@@ -367,7 +380,7 @@
     bf16, f32 = jnp.bfloat16, jnp.float32
     blocks = rows * nq // LANES
     return pl.pallas_call(
-        functools.partial(kernel, n, rows, chunks // 2),
+        functools.partial(kernel, n, rows, 4, 4),
         out_shape=jax.ShapeDtypeStruct((1, nq, HD), bf16),
         in_specs=[hbm] * 10,
         out_specs=vmem,

time: 21.9 us -> 21.6 us (0.986)
  Pallas kernels: 20.4 us -> 20.1 us
    pallas_call x1, Pallas kernels: 20.4 us -> 20.1 us  [local(): pl.pallas_call(functools.partial(kernel, n, rows, 4, 4), out_shape=jax.Sh...]
where the time goes in v3:
time: 21.6 us; the launch traced here: 21.4 us
  Pallas kernels  20.1 us (93%)
  local copies, waits for them, and re-layouts  1.3 us (6%)
    pallas_call x1, Pallas kernels, local(): pl.pallas_call(functools.partial(kernel, n, rows, 4, 4), out_shape=jax.Sh...  20.1 us
    unnamed x1, local copies, waits for them, and re-layouts  1.3 us

profile of v3, /device:TPU:0, one launch (start us, length us, event | category | flops | bytes accessed | tf_op | source)
XLA Modules:
  0.0 21.4 jit_solution(12546892249568175648)
XLA Ops:
  0.0 20.1 %shard_map.100 = bf16[1,32,128]{2,1,0:T(8,128)(2,1)} custom-call(s32[8]{0:T(128)} %lengths_hbm.1, s32[8]{0:T(128)} %dest_hbm.1, bf16[288,5120]{1,0:T(8,128)(2,1)} %hidden.1, bf16[5120,512]{1,0:T(8,128)(2,1)} %key_weight.1, bf16[5120,512]{1,0:T(8,128)(2,1)} %value_weight.1, f32[1,128]{1,0:T(1,128)} %bitcast.1, f32[1,128]{1,0:T(1,128)} %constant.2.clone.freq_hbm, ...), custom_call_target="tpu_custom_call" | custom-call | tf_op jit(solution)/shard_map/pallas_call | solution.py:382
  20.1 1.3 %copy.12 = bf16[1,32,128]{2,1,0:T(8,128)(2,1)} copy(bf16[1,32,128]{2,1,0:T(8,128)(2,1)} %shard_map.100) | data formatting | bytes 16384
